TPU v7x, 256 devices: a whole 4x4x8 slice. The times are simulated.
256 devices in a mesh: tup: 32 (over z, y), lang: 8 (over x, core).
Axes of the slice: x: 4, y: 4, z: 8, core: 2. Of those that a mesh axis runs over, the one named last changes fastest.
Arguments:
- counts: bfloat16 [8, 4096, 16384], P('lang', 'tup'), may hold values from 0 to 80
- lengths: int32 [8, 4096], P('lang', 'tup'), may hold values from 96 to 128, as said below
- tuple_map: int32 [8, 4096], P('lang', 'tup'), may hold values from 0 to 4095, as said below
- topic_mix: bfloat16 [4096, 256], P('tup'), may hold values from 0.049804688 to 5
- word_probs: bfloat16 [8, 16384, 256], P('lang', 'tup'), may hold values from 0.099609375 to 10
Outputs:
- mix_update: float32 [4096, 256], P('tup')
- word_update: float32 [8, 16384, 256], P('lang', 'tup')
Inputs may be any that keep to these rules, and one draw needn't show every extreme that they name: `lengths`: the first row of every language spans all 128 tiles. `tuple_map`: each language names every tuple once; the 128 rows of one index of tup hold exactly 4 tuples t of each value of t // 128.
All inputs are finite; a program needn't handle non-finite values.
Results may differ from a plain program's by a relative error of at most 0.0003.
Values may be sent and summed in bfloat16 or wider, within the bound.
No kernel may reach another device: no remote copies, remote signals or barrier semaphores. Data moves between devices by JAX's collectives and lax.ppermute only.
A program may use at most 128 MiB of HBM per device.

v0:
```python
import math
import jax
import jax.numpy as jnp
from jax import lax
from jax.sharding import PartitionSpec as P


def ratio_block(count_block, mix_block, word_block):
    expected = lax.dot_general(
        mix_block, word_block, (((1,), (1,)), ((), ())), preferred_element_type=jnp.float32
    )
    return count_block.astype(jnp.float32) / expected


def topic_term(ratios, word_block):
    return jnp.dot(ratios, word_block.astype(jnp.float32), precision=lax.Precision.HIGHEST)


def word_term(ratios, mix_rows):
    return lax.dot_general(
        ratios,
        mix_rows.astype(jnp.float32),
        (((0,), (0,)), ((), ())),
        precision=lax.Precision.HIGHEST,
    )


def ratio_pass(row_counts, mix_rows, word_local):
    shard_len = word_local.shape[0]
    topics = word_local.shape[1]
    vocab_size = shard_len * lax.axis_size("tup")
    topic_zero = jnp.zeros((row_counts.shape[0], topics), jnp.float32)
    shard_rows = lax.all_gather(word_local, "tup", axis=0, tiled=True)
    row_span = shard_rows.shape[0]
    block_len = math.gcd(row_span, 2048)

    def block_step(block_index, inner_pair):
        topic_sum, word_sum = inner_pair
        begin_row = block_index * block_len
        word_block = lax.dynamic_slice_in_dim(shard_rows, begin_row, block_len, 0)
        count_block = lax.dynamic_slice_in_dim(row_counts, begin_row, block_len, 1)
        ratios = ratio_block(count_block, mix_rows, word_block)
        topic_sum = topic_sum + topic_term(ratios, word_block)
        word_sum = lax.dynamic_update_slice_in_dim(
            word_sum, word_term(ratios, mix_rows), begin_row, 0
        )
        return (topic_sum, word_sum)

    topic_sum, word_sum = lax.fori_loop(
        0,
        row_span // block_len,
        block_step,
        (topic_zero, jnp.zeros((vocab_size, topics), jnp.float32)),
    )
    return (topic_sum, lax.psum_scatter(word_sum, "tup", scatter_dimension=0, tiled=True))


def on_device(counts, lengths, tuple_map, topic_mix, word_probs):
    count_rows = counts[0]
    tup_rows, vocab_size = count_rows.shape
    topics = topic_mix.shape[1]
    groups = lax.axis_size("tup")
    per_owner = tup_rows // groups
    tile_of = jnp.arange(vocab_size, dtype=jnp.int32) // 128
    live_counts = count_rows * (tile_of[None, :] < lengths[0][:, None]).astype(jnp.bfloat16)
    tuple_ids = tuple_map[0]
    word_local = word_probs[0]
    bucket_order = jnp.argsort(tuple_ids // tup_rows, stable=True)
    bucket_ids = tuple_ids[bucket_order].reshape(groups, per_owner)
    arrived = lax.all_to_all(
        live_counts[bucket_order].reshape(groups, per_owner, vocab_size),
        "tup",
        split_axis=0,
        concat_axis=0,
        tiled=True,
    ).reshape(tup_rows, vocab_size)
    arrived_ids = lax.all_to_all(
        bucket_ids, "tup", split_axis=0, concat_axis=0, tiled=True
    ).reshape(tup_rows)
    local_ids = arrived_ids % tup_rows
    mix_rows = topic_mix[local_ids]
    topic_sum, word_sum = ratio_pass(arrived, mix_rows, word_local)
    placed = jnp.zeros_like(topic_sum).at[local_ids].set(topic_sum)
    totals = lax.psum(placed, "lang")
    mixed = topic_mix.astype(jnp.float32) * totals
    mix_update = topics * mixed / jnp.sum(mixed, 1, keepdims=True)
    scaled = word_local.astype(jnp.float32) * word_sum
    column = lax.psum(jnp.sum(scaled, 0), "tup")
    word_update = (vocab_size * scaled / column[None, :])[None]
    return (mix_update, word_update)


def solution(mesh):
    return jax.shard_map(
        on_device,
        mesh=mesh,
        in_specs=(
            P("lang", "tup", None),
            P("lang", "tup"),
            P("lang", "tup"),
            P("tup", None),
            P("lang", "tup", None),
        ),
        out_specs=(P("tup", None), P("lang", "tup", None)),
        check_vma=False,
    )
```

profile of v0, /device:TPU:4, one launch (start us, length us, event | category | flops | bytes accessed | tf_op | source)
XLA Modules:
  0.0 659.9 jit_solution(987465419086488916)
XLA Ops:
  8.6 2.5 sort.17
  11.1 1.6 gather_fusion
  13.4 11.5 %all-to-all-start = ((s32[32,1,4]{2,1,0:T(1,128)}), s32[32,1,4]{2,1,0:T(1,128)S(1)}, u32[]{:S(2)}, u32[]{:S(2)}) async-start(s32[32,1,4]{2,1,0:T(1,128)} %bitcast.1), calls=%async_computation | async-start | bytes 32768 | tf_op jit(solution)/shard_map/all_to_all | solution.py:77
  24.9 5.4 compare_select_fusion
  30.3 11.5 %gather_fusion.1 = bf16[128,16384]{1,0:T(8,128)(2,1)} fusion(bf16[128,16384]{1,0:T(8,128)(2,1)} %compare_select_fusion, s32[1024]{0:T(1024)S(1)} %pad_clamp_fusion.1), kind=kCustom, calls=%fused_computation.1 | custom fusion | bytes 8389120 | tf_op jit(solution)/shard_map/gather | solution.py:71
  41.8 7.2 %reshape.96 = bf16[32,4,16384]{2,1,0:T(4,128)(2,1)} reshape(bf16[128,16384]{1,0:T(8,128)(2,1)} %gather_fusion.1) | data formatting | bytes 8388608 | tf_op jit(solution)/shard_map/reshape | solution.py:71
  49.1 10.0 %all-to-all-start.1 = ((bf16[32,4,16384]{2,1,0:T(4,128)(2,1)}), bf16[32,4,16384]{2,1,0:T(4,128)(2,1)}, u32[]{:S(2)}, u32[]{:S(2)}) async-start(bf16[32,4,16384]{2,1,0:T(4,128)(2,1)} %reshape.96), calls=%async_computation.1 | async-start | bytes 8388608 | tf_op jit(solution)/shard_map/all_to_all | solution.py:70
  61.6 130.7 %all-to-all-done.1 = bf16[32,4,16384]{2,1,0:T(4,128)(2,1)} async-done(((bf16[32,4,16384]{2,1,0:T(4,128)(2,1)}), bf16[32,4,16384]{2,1,0:T(4,128)(2,1)}, u32[]{:S(2)}, u32[]{:S(2)}) %all-to-all-start.1) | async-done | bytes 4194336 | tf_op jit(solution)/shard_map/all_to_all | solution.py:70
  192.2 6.9 %reshape.97 = bf16[128,16384]{1,0:T(8,128)(2,1)} reshape(bf16[32,4,16384]{2,1,0:T(4,128)(2,1)} %all-to-all-done.1) | data formatting | bytes 8388608 | tf_op jit(solution)/shard_map/reshape | solution.py:76
  199.2 6.0 broadcast_in_dim.7
  205.2 60.9 %while.16 = (s32[]{:T(128)}, f32[128,256]{1,0:T(8,128)S(1)}, f32[16384,256]{1,0:T(8,128)}, bf16[128,16384]{1,0:T(8,128)(2,1)}, bf16[16384,256]{1,0:T(8,128)(2,1)...) while((s32[]{:T(128)}, f32[128,256]{1,0:T(8,128)S(1)}, ...), condition=%wide.region_2.3_spmd.clone, body=%wide.region_1.2_spmd.clone.sunk | while | flops 1745420288 | bytes 10354869 | solution.py:49
  205.2 1.1 constant_dynamic-slice_fusion.2
  206.5 1.7 fusion.31
  208.2 2.3 convolution_add_fusion.2
  210.4 2.3 convolution_dynamic-update-slice_fusion.2
  212.8 1.1 constant_dynamic-slice_fusion.2
  214.1 1.7 fusion.31
  215.8 2.3 convolution_add_fusion.2
  218.1 2.3 convolution_dynamic-update-slice_fusion.2
  220.3 1.1 constant_dynamic-slice_fusion.2
  221.7 1.7 fusion.31
  223.4 2.3 convolution_add_fusion.2
  225.6 2.3 convolution_dynamic-update-slice_fusion.2
  227.9 1.1 constant_dynamic-slice_fusion.2
  229.3 1.7 fusion.31
  231.0 2.3 convolution_add_fusion.2
  233.2 2.3 convolution_dynamic-update-slice_fusion.2
  235.6 1.1 constant_dynamic-slice_fusion.2
  236.9 1.7 fusion.31
  238.6 2.3 convolution_add_fusion.2
  240.9 2.4 convolution_dynamic-update-slice_fusion.2
  243.2 1.1 constant_dynamic-slice_fusion.2
  244.6 1.7 fusion.31
  246.3 2.3 convolution_add_fusion.2
  248.5 2.3 convolution_dynamic-update-slice_fusion.2
  252.2 1.7 fusion.31
  253.8 2.3 convolution_add_fusion.2
  256.1 2.3 convolution_dynamic-update-slice_fusion.2
  259.8 1.7 fusion.31
  261.5 2.3 convolution_add_fusion.2
  263.7 2.3 convolution_dynamic-update-slice_fusion.2
  266.0 1.6 scatter_custom_fusion
  268.4 57.4 %all-reduce.2.cloned.1.call-done = f32[128,256]{1,0:T(8,128)} async-done(((f32[128,256]{1,0:T(8,128)}), f32[128,256]{1,0:T(8,128)}) %all-reduce.2.cloned.1.call-update) | async-done | bytes 131088 | tf_op jit(solution)/shard_map/psum | solution.py:84
  326.8 1.7 multiply_divide_fusion
  328.5 249.4 %reduce-scatter.2.cloned.1.call-done = f32[512,256]{1,0:T(8,128)} async-done(((f32[16384,256]{1,0:T(8,128)}), f32[512,256]{1,0:T(8,128)}) %reduce-scatter.2.cloned.1.call-update) | async-done | bytes 524304 | tf_op jit(solution)/shard_map/reduce_scatter | solution.py:55
  577.9 1.1 fusion.5
  579.1 72.4 %psum.15 = f32[256]{0:T(256)S(1)} all-reduce(f32[256]{0:T(256)S(1)} %fusion.5), channel_id=1, replica_groups=mesh['tup'=32,'lang'=8] {'tup'}, use_global_device_ids=true, to_apply=%region_8.9 | all-reduce | flops 256 | bytes 2048 | tf_op jit(solution)/shard_map/psum | solution.py:88
  651.5 1.9 divide_bitcast_fusion
  (36 shorter events, 10.6 us)
Async XLA Ops:
  7.2 192.0 %all-gather.3.cloned.1.call-start = ((), (), s32[]{:S(2)}) async-start(), calls=%async_computation.5 | async-start | bytes 8650752 | tf_op jit(solution)/shard_map/all_gather | solution.py:33
  13.4 35.6 %all-to-all-start = ((s32[32,1,4]{2,1,0:T(1,128)}), s32[32,1,4]{2,1,0:T(1,128)S(1)}, u32[]{:S(2)}, u32[]{:S(2)}) async-start(s32[32,1,4]{2,1,0:T(1,128)} %bitcast.1), calls=%async_computation | async-start | bytes 32768 | tf_op jit(solution)/shard_map/all_to_all | solution.py:77
  49.1 11.6 %copy-start = (bf16[128,256]{1,0:T(8,128)(2,1)S(1)}, bf16[128,256]{1,0:T(8,128)(2,1)}, u32[]{:S(2)}) copy-start(bf16[128,256]{1,0:T(8,128)(2,1)} %param.10) | copy-start | bytes 196612
  49.1 143.2 %all-to-all-start.1 = ((bf16[32,4,16384]{2,1,0:T(4,128)(2,1)}), bf16[32,4,16384]{2,1,0:T(4,128)(2,1)}, u32[]{:S(2)}, u32[]{:S(2)}) async-start(bf16[32,4,16384]{2,1,0:T(4,128)(2,1)} %reshape.96), calls=%async_computation.1 | async-start | bytes 8388608 | tf_op jit(solution)/shard_map/all_to_all | solution.py:70
  59.1 266.7 %all-reduce.2.cloned.1.call-start = ((), (), s32[]{:S(2)}) async-start(), calls=%async_computation.3 | async-start | bytes 262144 | tf_op jit(solution)/shard_map/psum | solution.py:84
  267.7 310.2 %reduce-scatter.2.cloned.1.call-start = ((), (), s32[]{:S(2)}) async-start(), calls=%async_computation.4 | async-start | bytes 17301504 | tf_op jit(solution)/shard_map/reduce_scatter | solution.py:55
  267.7 310.2 %copy-start.1 = (bf16[1,512,256]{2,1,0:T(8,128)(2,1)S(1)}, bf16[1,512,256]{2,1,0:T(8,128)(2,1)}, u32[]{:S(2)}) copy-start(bf16[1,512,256]{2,1,0:T(8,128)(2,1)} %param.11) | copy-start | bytes 786436
Sparse Core Ops, SparseCore 0:
  10.6 176.9 all-gather.2
  267.8 57.9 all-reduce.1
  330.5 247.3 reduce-scatter.1
where the time goes:
time: 662 us; the launch traced here: 660 us
  waiting for transfers between devices  439 us (66%)
  blocking collectives  72.4 us (11%)
  matrix products  49.9 us (8%)
  local copies, waits for them, and re-layouts  47.8 us (7%)
  starting transfers between devices  21.8 us (3%)
  other arithmetic  15.1 us (2%)
  between operations  13.8 us (2%)
    reduce_scatter x1, waiting for transfers between devices, ratio_pass(): lax.psum_scatter(word_sum, 'tup', scatter_dimension=0, tiled=True)  249 us
    all_to_all x1, waiting for transfers between devices, on_device(): lax.all_to_all(live_counts[bucket_order].reshape(groups, per_owner, vocab...  131 us
    psum x1, blocking collectives, on_device(): column = lax.psum(jnp.sum(scaled, 0), 'tup')  72.4 us
    psum x1, waiting for transfers between devices, on_device(): totals = lax.psum(placed, 'lang')  57.4 us
    dot_general x8, matrix products, word_term(): lax.dot_general(ratios, mix_rows.astype(jnp.float32), (((0,), (0,)), ((),...  18.6 us
    dot_general x8, matrix products, topic_term(): jnp.dot(ratios, word_block.astype(jnp.float32), precision=lax.Precision.H...  18 us
    dot_general x8, matrix products, ratio_block(): lax.dot_general(mix_block, word_block, (((1,), (1,)), ((), ())), preferre...  13.3 us
  transfers between devices with their start and end apart: 5, of which 3 were waited for; matrix products, arithmetic and copies ran while one was open for 6% of the time, Pallas kernels for 0%

commit v1 on v0

--- a/solution.py
+++ b/solution.py
@@ -81,7 +81,9 @@
     mix_rows = topic_mix[local_ids]
     topic_sum, word_sum = ratio_pass(arrived, mix_rows, word_local)
     placed = jnp.zeros_like(topic_sum).at[local_ids].set(topic_sum)
-    totals = lax.psum(placed, "lang")
+    totals = placed
+    for hop in (1, 2, 4):
+        totals = totals + lax.ppermute(totals, "lang", [(dev, dev ^ hop) for dev in range(8)])
     mixed = topic_mix.astype(jnp.float32) * totals
     mix_update = topics * mixed / jnp.sum(mixed, 1, keepdims=True)
     scaled = word_local.astype(jnp.float32) * word_sum

time: 662 us -> 592 us (0.89)
  waiting for transfers between devices: 439 us -> 370 us
    psum x1 -> x0, waiting for transfers between devices: 57.4 us -> none  [on_device(): totals = lax.psum(placed, 'lang')]
    reduce_scatter x1, waiting for transfers between devices: 249 us -> 227 us  [ratio_pass(): lax.psum_scatter(word_sum, 'tup', scatter_dimension=0, tiled=True)]
    ppermute x0 -> x3, waiting for transfers between devices: none -> 11.6 us  [on_device(): lax.ppermute(totals, 'lang', [(dev, dev ^ hop) for dev in range(8)])]
  transfers between devices with their start and end apart: 5 -> 7, of which waited for: 3 -> 5; matrix products, arithmetic and copies ran while one was open for 6% -> 7% of each run, Pallas kernels for 0% -> 0%
where the time goes in v1:
time: 592 us; the launch traced here: 590 us
  waiting for transfers between devices  370 us (62%)
  blocking collectives  72.2 us (12%)
  matrix products  49.9 us (8%)
  local copies, waits for them, and re-layouts  47.2 us (8%)
  starting transfers between devices  23.8 us (4%)
  between operations  14.1 us (2%)
  other arithmetic  13.3 us (2%)
    reduce_scatter x1, waiting for transfers between devices, ratio_pass(): lax.psum_scatter(word_sum, 'tup', scatter_dimension=0, tiled=True)  227 us
    all_to_all x1, waiting for transfers between devices, on_device(): lax.all_to_all(live_counts[bucket_order].reshape(groups, per_owner, vocab...  131 us
    psum x1, blocking collectives, on_device(): column = lax.psum(jnp.sum(scaled, 0), 'tup')  72.2 us
    dot_general x8, matrix products, word_term(): lax.dot_general(ratios, mix_rows.astype(jnp.float32), (((0,), (0,)), ((),...  18.6 us
    dot_general x8, matrix products, topic_term(): jnp.dot(ratios, word_block.astype(jnp.float32), precision=lax.Precision.H...  18 us
    dot_general x8, matrix products, ratio_block(): lax.dot_general(mix_block, word_block, (((1,), (1,)), ((), ())), preferre...  13.3 us
  transfers between devices with their start and end apart: 7, of which 5 were waited for; matrix products, arithmetic and copies ran while one was open for 7% of the time, Pallas kernels for 0%

profile of v1, /device:TPU:4, one launch (start us, length us, event | category | flops | bytes accessed | tf_op | source)
XLA Modules:
  0.0 590.3 jit_solution(16640952156614752253)
XLA Ops:
  8.6 2.5 sort.17
  11.1 1.6 gather_fusion
  13.4 11.5 %all-to-all-start = ((s32[32,1,4]{2,1,0:T(1,128)}), s32[32,1,4]{2,1,0:T(1,128)S(1)}, u32[]{:S(2)}, u32[]{:S(2)}) async-start(s32[32,1,4]{2,1,0:T(1,128)} %bitcast.1), calls=%async_computation | async-start | bytes 32768 | tf_op jit(solution)/shard_map/all_to_all | solution.py:77
  24.9 5.4 compare_select_fusion
  30.3 11.5 %gather_fusion.1 = bf16[128,16384]{1,0:T(8,128)(2,1)} fusion(bf16[128,16384]{1,0:T(8,128)(2,1)} %compare_select_fusion, s32[1024]{0:T(1024)S(1)} %pad_clamp_fusion.1), kind=kCustom, calls=%fused_computation.1 | custom fusion | bytes 8389120 | tf_op jit(solution)/shard_map/gather | solution.py:71
  41.8 7.2 %reshape.96 = bf16[32,4,16384]{2,1,0:T(4,128)(2,1)} reshape(bf16[128,16384]{1,0:T(8,128)(2,1)} %gather_fusion.1) | data formatting | bytes 8388608 | tf_op jit(solution)/shard_map/reshape | solution.py:71
  49.1 10.0 %all-to-all-start.1 = ((bf16[32,4,16384]{2,1,0:T(4,128)(2,1)}), bf16[32,4,16384]{2,1,0:T(4,128)(2,1)}, u32[]{:S(2)}, u32[]{:S(2)}) async-start(bf16[32,4,16384]{2,1,0:T(4,128)(2,1)} %reshape.96), calls=%async_computation.1 | async-start | bytes 8388608 | tf_op jit(solution)/shard_map/all_to_all | solution.py:70
  61.6 130.7 %all-to-all-done.1 = bf16[32,4,16384]{2,1,0:T(4,128)(2,1)} async-done(((bf16[32,4,16384]{2,1,0:T(4,128)(2,1)}), bf16[32,4,16384]{2,1,0:T(4,128)(2,1)}, u32[]{:S(2)}, u32[]{:S(2)}) %all-to-all-start.1) | async-done | bytes 4194336 | tf_op jit(solution)/shard_map/all_to_all | solution.py:70
  192.2 6.9 %reshape.97 = bf16[128,16384]{1,0:T(8,128)(2,1)} reshape(bf16[32,4,16384]{2,1,0:T(4,128)(2,1)} %all-to-all-done.1) | data formatting | bytes 8388608 | tf_op jit(solution)/shard_map/reshape | solution.py:76
  199.2 6.0 %broadcast_in_dim.7 = f32[16384,256]{1,0:T(8,128)} broadcast(f32[]{:T(128)} %constant.70.clone.1), dimensions={} | broadcast | bytes 16777220 | tf_op jit(solution)/shard_map/broadcast_in_dim | solution.py:53
  205.2 60.9 %while.16 = (s32[]{:T(128)}, f32[128,256]{1,0:T(8,128)S(1)}, f32[16384,256]{1,0:T(8,128)}, bf16[128,16384]{1,0:T(8,128)(2,1)}, bf16[16384,256]{1,0:T(8,128)(2,1)...) while((s32[]{:T(128)}, f32[128,256]{1,0:T(8,128)S(1)}, ...), condition=%wide.region_2.3_spmd.clone, body=%wide.region_1.2_spmd.clone.sunk | while | flops 1745420288 | bytes 10354869 | solution.py:49
  205.2 1.1 constant_dynamic-slice_fusion.2
  206.5 1.7 fusion.31
  208.2 2.3 convolution_add_fusion.2
  210.4 2.3 convolution_dynamic-update-slice_fusion.2
  212.8 1.1 constant_dynamic-slice_fusion.2
  214.1 1.7 fusion.31
  215.8 2.3 convolution_add_fusion.2
  218.1 2.3 convolution_dynamic-update-slice_fusion.2
  220.3 1.1 constant_dynamic-slice_fusion.2
  221.7 1.7 fusion.31
  223.4 2.3 convolution_add_fusion.2
  225.6 2.3 convolution_dynamic-update-slice_fusion.2
  227.9 1.1 constant_dynamic-slice_fusion.2
  229.3 1.7 fusion.31
  231.0 2.3 convolution_add_fusion.2
  233.2 2.3 convolution_dynamic-update-slice_fusion.2
  235.6 1.1 constant_dynamic-slice_fusion.2
  236.9 1.7 fusion.31
  238.6 2.3 convolution_add_fusion.2
  240.9 2.4 convolution_dynamic-update-slice_fusion.2
  244.6 1.7 fusion.31
  246.3 2.3 convolution_add_fusion.2
  248.5 2.3 convolution_dynamic-update-slice_fusion.2
  252.2 1.7 fusion.31
  253.8 2.3 convolution_add_fusion.2
  256.1 2.3 convolution_dynamic-update-slice_fusion.2
  259.8 1.7 fusion.31
  261.5 2.3 convolution_add_fusion.2
  263.7 2.3 convolution_dynamic-update-slice_fusion.2
  267.2 1.3 collective-permute-done
  268.6 1.3 collective-permute-start.1
  269.9 4.3 collective-permute-done.1
  274.8 6.0 %collective-permute-done.2 = f32[128,256]{1,0:T(8,128)S(1)} collective-permute-done((f32[128,256]{1,0:T(8,128)S(1)}, f32[128,256]{1,0:T(8,128)S(1)}, u32[]{:S(2)}, u32[]{:S(2)}) %collective-permute-start.2) | collective-permute-done | bytes 131104 | tf_op jit(solution)/shard_map/ppermute | solution.py:86
  281.7 226.6 %reduce-scatter.2.cloned.1.call-done = f32[512,256]{1,0:T(8,128)} async-done(((f32[16384,256]{1,0:T(8,128)}), f32[512,256]{1,0:T(8,128)}) %reduce-scatter.2.cloned.1.call-update) | async-done | bytes 524304 | tf_op jit(solution)/shard_map/reduce_scatter | solution.py:55
  508.2 1.1 fusion.5
  509.4 72.2 %psum.7 = f32[256]{0:T(256)S(1)} all-reduce(f32[256]{0:T(256)S(1)} %fusion.5), channel_id=1, replica_groups=mesh['tup'=32,'lang'=8] {'tup'}, use_global_device_ids=true, to_apply=%region_7.8 | all-reduce | flops 256 | bytes 2048 | tf_op jit(solution)/shard_map/psum | solution.py:90
  581.6 1.9 divide_bitcast_fusion
  (41 shorter events, 12.6 us)
Async XLA Ops:
  7.2 192.0 %all-gather.3.cloned.1.call-start = ((), (), s32[]{:S(2)}) async-start(), calls=%async_computation.4 | async-start | bytes 8650752 | tf_op jit(solution)/shard_map/all_gather | solution.py:33
  13.4 35.6 %all-to-all-start = ((s32[32,1,4]{2,1,0:T(1,128)}), s32[32,1,4]{2,1,0:T(1,128)S(1)}, u32[]{:S(2)}, u32[]{:S(2)}) async-start(s32[32,1,4]{2,1,0:T(1,128)} %bitcast.1), calls=%async_computation | async-start | bytes 32768 | tf_op jit(solution)/shard_map/all_to_all | solution.py:77
  49.1 11.6 %copy-start = (bf16[128,256]{1,0:T(8,128)(2,1)S(1)}, bf16[128,256]{1,0:T(8,128)(2,1)}, u32[]{:S(2)}) copy-start(bf16[128,256]{1,0:T(8,128)(2,1)} %param.10) | copy-start | bytes 196612
  49.1 143.2 %all-to-all-start.1 = ((bf16[32,4,16384]{2,1,0:T(4,128)(2,1)}), bf16[32,4,16384]{2,1,0:T(4,128)(2,1)}, u32[]{:S(2)}, u32[]{:S(2)}) async-start(bf16[32,4,16384]{2,1,0:T(4,128)(2,1)} %reshape.96), calls=%async_computation.1 | async-start | bytes 8388608 | tf_op jit(solution)/shard_map/all_to_all | solution.py:70
  59.1 449.1 %reduce-scatter.2.cloned.1.call-start = ((), (), s32[]{:S(2)}) async-start(), calls=%async_computation.3 | async-start | bytes 17301504 | tf_op jit(solution)/shard_map/reduce_scatter | solution.py:55
  266.0 242.2 %copy-start.1 = (bf16[1,512,256]{2,1,0:T(8,128)(2,1)S(1)}, bf16[1,512,256]{2,1,0:T(8,128)(2,1)}, u32[]{:S(2)}) copy-start(bf16[1,512,256]{2,1,0:T(8,128)(2,1)} %param.11) | copy-start | bytes 786436
  267.1 1.4 collective-permute-start
  268.6 5.6 collective-permute-start.1
  274.2 6.6 %collective-permute-start.2 = (f32[128,256]{1,0:T(8,128)S(1)}, f32[128,256]{1,0:T(8,128)S(1)}, u32[]{:S(2)}, u32[]{:S(2)}) collective-permute-start(f32[128,256]{1,0:T(8,128)S(1)} %add.83), channel_id=1, source_target_pairs={{0,4},{1,5},{2,6},{3,7},{4,0},{5,1},{6,2},{7,3},{8,12},{9,13},{10,... | collective-permute-start | bytes 393224 | tf_op jit(solution)/shard_map/ppermute | solution.py:86
Sparse Core Ops, SparseCore 0:
  10.6 176.9 all-gather.2
  266.2 242.0 reduce-scatter.1
